TPU v7x, 32 devices: a whole 2x2x4 slice. The times are simulated.
32 devices in a mesh: groups: 2 (over y), bundle: 16 (over z, x, core).
Axes of the slice: x: 2, y: 2, z: 4, core: 2. Of those that a mesh axis runs over, the one named last changes fastest.
Arguments:
- objective: float32 [512, 8192], P(('groups', 'bundle')), parts along dimension 0, may hold values from -8 to 8
- demands: float32 [512, 8192], P(('groups', 'bundle')), parts along dimension 0, may hold values from -6 to 6
- multipliers: float32 [512, 6144], P(('groups', 'bundle')), parts along dimension 0, may hold values from -4 to 4
- probability: float32 [512], P(('groups', 'bundle')), parts along dimension 0, may hold values from 1 to 9
- matrix_tiles: bfloat16 [512, 128, 128], P('groups'), parts along dimension 0, may hold values from -0.25 to 0.25
- tile_row: int32 [512], P('groups'), parts along dimension 0, may hold values from 0 to 63, as said below
- tile_col: int32 [512], P('groups'), parts along dimension 0, may hold values from 0 to 63
- unit_kind: int32 [16384], P('groups'), parts along dimension 0, may hold values 0 or 1
- leaf_node: int32 [512], P(('groups', 'bundle')), parts along dimension 0, may hold values from 0 to 63, as said below
- node_parent: int32 [128], P('groups'), parts along dimension 0, may hold values from 0 to 7, as said below
Outputs:
- solution: float32 [512, 8192], P(('groups', 'bundle')), parts along dimension 0
- new_multipliers: float32 [512, 6144], P(('groups', 'bundle')), parts along dimension 0
- hedging_gap: float32 [4], P('groups'), parts along dimension 0
- lagrange_bound: float32 [4], P('groups'), parts along dimension 0
There are 2 independent parts, one for each index of `groups`. A program takes and returns all parts, laid end to end along the dimension named above; each array names one. Nothing has to cross between parts.
Inputs may be any that keep to these rules, and one draw needn't show every extreme that they name: `leaf_node`: each of the 64 third-section nodes holds exactly 4 scenarios. `node_parent`: each second-section node is the parent of exactly 8 third-section nodes. `tile_row`: each tile row holds exactly 4 tiles.
All inputs are finite; a program needn't handle non-finite values.
Results may differ from a plain program's by a relative error of at most 0.0011.
Values sent between devices are 32-bit elements; how exact they have to be, the bound alone decides.
A program may use at most 128 MiB of HBM per device.

v0:
```python
import jax
import jax.numpy as jnp
from jax import lax
from jax.sharding import PartitionSpec as P

NODES2 = 8
ITERS = 2
PDHG_STEPS = 2


step_tau = 0.4
step_sigma = 0.4
penalty = 0.5


def forward(grouped_tiles, sorted_cols, vector):
    batch_size = vector.shape[0]
    con_blocks, per_row, tile_size = (
        grouped_tiles.shape[0],
        grouped_tiles.shape[1],
        grouped_tiles.shape[2],
    )
    blocks = vector.reshape(batch_size, -1, tile_size)
    picked = jnp.take(blocks, sorted_cols, axis=1).reshape(
        batch_size, con_blocks, per_row, tile_size
    )
    product = jnp.einsum(
        "rkij,srkj->sri", grouped_tiles, picked, preferred_element_type=jnp.float32
    )
    return product.reshape(batch_size, -1)


def backward(grouped_tiles, cols_onehot, vector):
    batch_size = vector.shape[0]
    con_blocks, per_row, tile_size = (
        grouped_tiles.shape[0],
        grouped_tiles.shape[1],
        grouped_tiles.shape[2],
    )
    blocks = vector.reshape(batch_size, con_blocks, tile_size)
    product = jnp.einsum(
        "rkij,sri->srkj", grouped_tiles, blocks, preferred_element_type=jnp.float32
    )
    product = product.reshape(batch_size, con_blocks * per_row, tile_size)
    summed = jnp.einsum("vt,stj->svj", cols_onehot, product, precision=lax.Precision.HIGH)
    return summed.reshape(batch_size, -1)


def shards(
    objective,
    demands,
    multipliers,
    probability,
    matrix_tiles,
    tile_row,
    tile_col,
    unit_kind,
    leaf_node,
    node_parent,
):
    scen_count = objective.shape[0]
    section_width = multipliers.shape[1] // 3
    tile_size = matrix_tiles.shape[1]
    var_blocks = objective.shape[1] // tile_size
    con_blocks = demands.shape[1] // tile_size
    tile_order = jnp.argsort(tile_row, stable=True)
    grouped_tiles = jnp.take(matrix_tiles, tile_order, axis=0).reshape(
        con_blocks, -1, tile_size, tile_size
    )
    sorted_cols = jnp.take(tile_col, tile_order)
    cols_onehot = (sorted_cols[None, :] == jnp.arange(var_blocks, dtype=jnp.int32)[:, None]).astype(
        jnp.float32
    )
    upper = jnp.where(unit_kind == 1, 1.0, 3.0).astype(jnp.float32)
    member_three = (
        leaf_node[:, None] == jnp.arange(node_parent.shape[0], dtype=jnp.int32)[None, :]
    ).astype(jnp.float32)
    parent_map = (node_parent[:, None] == jnp.arange(NODES2, dtype=jnp.int32)[None, :]).astype(
        jnp.float32
    )
    member_two = jnp.dot(member_three, parent_map, precision=lax.Precision.HIGHEST)
    member_one = jnp.ones((scen_count, 1), jnp.float32)
    members = (member_one, member_two, member_three)
    local_weights = jnp.concatenate(
        [jnp.dot(probability, member, precision=lax.Precision.HIGHEST) for member in members]
    )
    node_totals = lax.psum(local_weights, "bundle")
    total_prob = node_totals[0]
    weight_flat = jnp.repeat(node_totals, section_width)
    zeros_section = jnp.zeros((scen_count, section_width), jnp.float32)

    def primal_dual(primal, dual, linear, anchor, dual_back):
        if dual_back is None:
            dual_back = backward(grouped_tiles, cols_onehot, dual.astype(jnp.bfloat16))
        gradient = linear + dual_back
        if anchor is not None:
            gradient = gradient + penalty * jnp.concatenate(
                [primal[:, : 3 * section_width] - anchor, zeros_section], axis=1
            )
        moved = jnp.clip(primal - step_tau * gradient, 0.0, upper)
        image = forward(grouped_tiles, sorted_cols, (2.0 * moved - primal).astype(jnp.bfloat16))
        return (moved, jnp.maximum(dual + step_sigma * (image - demands), 0.0))

    primal = jnp.zeros_like(objective)
    dual = jnp.zeros_like(demands)
    spoke_primal = primal
    spoke_dual = dual
    weights_now = multipliers
    anchor = None
    hub_back = None
    spoke_back = None
    gap_terms = []
    bound_terms = []
    for iteration in range(ITERS):
        linear = objective + jnp.concatenate([weights_now, zeros_section], axis=1)
        for inner in range(PDHG_STEPS):
            primal, dual = primal_dual(
                primal, dual, linear, anchor, hub_back if inner == 0 else None
            )
        hub_back = None
        pieces = []
        for section_index in range(3):
            consensus_member = members[section_index]
            part_values = primal[
                :, section_index * section_width : (section_index + 1) * section_width
            ]
            weighted = consensus_member * probability[:, None]
            pieces.append(
                jnp.dot(weighted.T, part_values, precision=lax.Precision.HIGHEST).reshape(-1)
            )
        flat_sums = jnp.concatenate(pieces)
        mean_values = lax.psum(flat_sums, "bundle") / weight_flat
        result = []
        offset = 0
        for consensus_member in members:
            node_count = consensus_member.shape[1]
            node_table = mean_values[offset : offset + node_count * section_width].reshape(
                node_count, section_width
            )
            result.append(jnp.dot(consensus_member, node_table, precision=lax.Precision.HIGHEST))
            offset = offset + node_count * section_width
        agreed = jnp.concatenate(result, axis=1)
        deviation = primal[:, : 3 * section_width] - agreed
        gap_term = jnp.sum(probability * jnp.sum(deviation * deviation, axis=1))
        if iteration == 0:
            spoke_primal, spoke_dual = (primal, dual)
        else:
            for inner in range(PDHG_STEPS):
                spoke_primal, spoke_dual = primal_dual(
                    spoke_primal, spoke_dual, linear, None, spoke_back if inner == 0 else None
                )
        spoke_back = backward(grouped_tiles, cols_onehot, spoke_dual.astype(jnp.bfloat16))
        if iteration == 0:
            hub_back = spoke_back
        reduced = linear + spoke_back
        bound_term = jnp.sum(
            probability
            * (jnp.sum(reduced * spoke_primal, axis=1) - jnp.sum(demands * spoke_dual, axis=1))
        )
        gap_terms.append(lax.psum(gap_term, "bundle"))
        bound_terms.append(lax.psum(bound_term, "bundle"))
        weights_now = weights_now + penalty * deviation
        anchor = agreed
    gap_totals = jnp.stack(gap_terms)
    bound_totals = jnp.stack(bound_terms)
    hedging_gap = gap_totals / (3 * section_width * total_prob)
    lagrange_bound = bound_totals / (objective.shape[1] * total_prob)
    return (primal, weights_now, hedging_gap, lagrange_bound)


def solution(mesh):
    in_specs = (
        P(("groups", "bundle"), None),
        P(("groups", "bundle"), None),
        P(("groups", "bundle"), None),
        P(("groups", "bundle")),
        P("groups", None, None),
        P("groups"),
        P("groups"),
        P("groups"),
        P(("groups", "bundle")),
        P("groups"),
    )
    out_specs = (
        P(("groups", "bundle"), None),
        P(("groups", "bundle"), None),
        P("groups"),
        P("groups"),
    )
    return jax.shard_map(shards, mesh=mesh, in_specs=in_specs, out_specs=out_specs, check_vma=False)
```

profile of v0, /device:TPU:1, one launch (start us, length us, event | category | flops | bytes accessed | tf_op | source)
XLA Modules:
  0.0 328.2 jit_solution(11985529887803379412)
XLA Ops:
  7.2 3.8 %sort.17 = (s32[256]{0:T(256)}, s32[256]{0:T(256)S(1)}) sort(s32[256]{0:T(256)} %param.17, s32[256]{0:T(256)S(1)} %iota.16), dimensions={0}, to_apply=%region_0.0 | sort | flops 2048 | bytes 4096 | tf_op jit(solution)/shard_map/jit(argsort)/sort | solution.py:66
  11.1 1.9 gather_fusion.1
  13.2 12.0 %gather_fusion = bf16[256,128,128]{2,1,0:T(8,128)(2,1)} fusion(bf16[256,128,128]{2,1,0:T(8,128)(2,1)} %param.16, s32[1024]{0:T(1024)S(1)} %pad_clamp_fusion.1), kind=kCustom, calls=%fused_computation.5 | custom fusion | bytes 16778240 | tf_op jit(solution)/shard_map/jit(_take)/gather | solution.py:67
  25.3 4.5 %fusion.66 = f32[64,16,4,128]{3,1,2,0:T(8,128)S(1)} fusion(bf16[64,4,128,128]{3,2,1,0:T(8,128)(2,1)} %bitcast.330, pred[64,4]{1,0:T(8,128)(4,1)S(1)} %broadcast_in_dim.60), kind=kOutput, calls=%fused_computation.128 | convolution fusion | flops 138412032 | bytes 10486016 | tf_op jit(solution)/shard_map/rkij,sri->srkj/dot_general | solution.py:41
  33.2 5.7 %convolution_bitcast_fusion.6 = f32[64,2,8,128]{3,2,1,0:T(8,128)S(1)} fusion(bf16[16,64,4,128]{3,0,2,1:T(8,128)(2,1)S(1)} %bitcast.373, bf16[64,4,128,128]{3,2,1,0:T(8,128)(2,1)} %bitcast.331, pred[64,4]{1,0:T(8,128)(4,1)} %copy-done.35), kind=kOutput, calls=%fused_computation.26 | convolution fusion | flops 138412032 | bytes 9961728 | tf_op jit(solution)/shard_map/rkij,srkj->sri/dot_general | solution.py:27
  39.1 2.1 fusion.64
  48.6 4.9 %convolution_bitcast_fusion.4 = f32[64,2,8,128]{3,2,1,0:T(8,128)S(1)} fusion(bf16[16,64,4,128]{3,0,2,1:T(8,128)(2,1)S(1)} %bitcast.374, bf16[64,4,128,128]{3,2,1,0:T(8,128)(2,1)} %bitcast.332, pred[64,4]{1,0:T(8,128)(4,1)S(1)} %copy-done.37), kind=kOutput, calls=%fused_computation.24 | convolution fusion | flops 138412032 | bytes 9961728 | tf_op jit(solution)/shard_map/rkij,srkj->sri/dot_general | solution.py:27
  54.6 3.0 fusion.62
  58.4 30.6 %psum.50 = f32[73]{0:T(128)S(1)} all-reduce(f32[73]{0:T(128)S(1)} %pad_maximum_fusion.3), channel_id=1, replica_groups=mesh['groups'=2,'bundle'=16] {'bundle'}, use_global_device_ids=true, to_apply=%region_2.4 | all-reduce | flops 73 | bytes 584 | tf_op jit(solution)/shard_map/psum | solution.py:87
  90.0 2.6 fusion.6
  92.6 46.2 %all-reduce.8.cloned.1.call-done = f32[149504]{0:T(1024)} async-done(((f32[149504]{0:T(1024)}), f32[149504]{0:T(1024)}) %all-reduce.8.cloned.1.call-update) | async-done | bytes 598032 | tf_op jit(solution)/shard_map/psum | solution.py:132
  142.2 2.0 fusion.95
  149.8 1.9 gather_fusion.5
  153.6 4.9 %convolution_bitcast_fusion.1 = f32[64,2,8,128]{3,2,1,0:T(8,128)S(1)} fusion(bf16[16,64,4,128]{3,0,2,1:T(8,128)(2,1)S(1)} %bitcast.375, bf16[64,4,128,128]{3,2,1,0:T(8,128)(2,1)} %bitcast.333, pred[64,4]{1,0:T(8,128)(4,1)} %copy-done.35), kind=kOutput, calls=%fused_computation.21 | convolution fusion | flops 138412032 | bytes 9961728 | tf_op jit(solution)/shard_map/rkij,srkj->sri/dot_general | solution.py:27
  159.6 2.0 fusion.58
  164.2 1.9 gather_fusion.6
  166.1 2.0 broadcast_select_fusion.1
  168.2 4.9 %convolution_bitcast_fusion = f32[64,2,8,128]{3,2,1,0:T(8,128)S(1)} fusion(bf16[16,64,4,128]{3,0,2,1:T(8,128)(2,1)S(1)} %bitcast.376, bf16[64,4,128,128]{3,2,1,0:T(8,128)(2,1)} %bitcast.334, pred[64,4]{1,0:T(8,128)(4,1)S(1)} %copy-done.38), kind=kOutput, calls=%fused_computation.20 | convolution fusion | flops 138412032 | bytes 9961728 | tf_op jit(solution)/shard_map/rkij,srkj->sri/dot_general | solution.py:27
  174.2 2.2 fusion.56
  182.7 4.9 %convolution_bitcast_fusion.3 = f32[64,2,8,128]{3,2,1,0:T(8,128)S(1)} fusion(bf16[16,64,4,128]{3,0,2,1:T(8,128)(2,1)S(1)} %bitcast.372, bf16[64,4,128,128]{3,2,1,0:T(8,128)(2,1)} %bitcast.335, pred[64,4]{1,0:T(8,128)(4,1)} %copy-done.35), kind=kOutput, calls=%fused_computation.23 | convolution fusion | flops 138412032 | bytes 9961728 | tf_op jit(solution)/shard_map/rkij,srkj->sri/dot_general | solution.py:27
  188.6 2.0 fusion.60
  194.4 90.9 %all-reduce.10.cloned.1.call-done = f32[149504]{0:T(1024)} async-done(((f32[149504]{0:T(1024)}), f32[149504]{0:T(1024)}) %all-reduce.10.cloned.1.call-update) | async-done | bytes 598032 | tf_op jit(solution)/shard_map/psum | solution.py:132
  289.0 29.3 %all-reduce.4 = (f32[1]{0:T(128)}, f32[1]{0:T(128)}, f32[1]{0:T(128)}, f32[1]{0:T(128)}) all-reduce(f32[1]{0:T(128)} %bitcast.43, f32[1]{0:T(128)} %bitcast.42, f32[1]{0:T(128)} %bitcast.64, f32[1]{0:T(128)} %bitcast.45), channel_id=1, replica_groups=mesh['groups'=2,'bundle'=16] {'bundle'}, use_global_device_ids=true, to_apply=%region_9.11 | all-reduce | flops 4 | bytes 32 | tf_op jit(solution)/shard_map/psum | solution.py:160
  318.3 3.1 maximum_divide_fusion
  (211 shorter events, 43.4 us)
Async XLA Ops:
  7.2 131.6 %all-reduce.8.cloned.1.call-start = ((), (), s32[]{:S(2)}) async-start(), calls=%async_computation | async-start | bytes 1196032 | tf_op jit(solution)/shard_map/psum | solution.py:132
  13.1 19.1 %copy-start.32 = (pred[256]{0:T(512)(128)(4,1)}, pred[256]{0:T(512)(128)(4,1)S(1)}, u32[]{:S(2)}) copy-start(pred[256]{0:T(512)(128)(4,1)S(1)} %get-tuple-element.29) | copy-start | bytes 772
  13.2 12.1 %copy-start.35 = (pred[64,4]{1,0:T(8,128)(4,1)}, pred[64,4]{1,0:T(8,128)(4,1)S(1)}, u32[]{:S(2)}) copy-start(pred[64,4]{1,0:T(8,128)(4,1)S(1)} %broadcast_in_dim.60) | copy-start | bytes 772
  30.8 8.0 %copy-start.31 = (s32[1024]{0:T(1024)}, s32[1024]{0:T(1024)S(1)}, u32[]{:S(2)}) copy-start(s32[1024]{0:T(1024)S(1)} %pad_clamp_fusion) | copy-start | bytes 12292
  31.3 7.5 %copy-start.1 = (f32[16,8192]{1,0:T(8,128)S(1)}, f32[16,8192]{1,0:T(8,128)}, u32[]{:S(2)}) copy-start(f32[16,8192]{1,0:T(8,128)} %param.13) | copy-start | bytes 1572868
  32.2 6.8 %slice-start = ((s8[8388608]{0:T(1024)(128)(4,1)}), s8[4194304]{0:T(1024)(128)(4,1)S(1)}, s32[]{:S(2)}) async-start(s8[8388608]{0:T(1024)(128)(4,1)} %bitcast.336), calls=%async_computation.2 | async-start | bytes 8388608
  32.2 6.8 %copy-start.36 = (pred[64,4]{1,0:T(8,128)(4,1)S(1)}, pred[64,4]{1,0:T(8,128)(4,1)}, u32[]{:S(2)}) copy-start(pred[64,4]{1,0:T(8,128)(4,1)} %copy-done.35) | copy-start | bytes 772
  41.1 6.5 %copy-start.33 = (pred[256]{0:T(512)(128)(4,1)S(1)}, pred[256]{0:T(512)(128)(4,1)}, u32[]{:S(2)}) copy-start(pred[256]{0:T(512)(128)(4,1)} %copy-done.32) | copy-start | bytes 772
  41.1 7.4 %copy-start.37 = (pred[64,4]{1,0:T(8,128)(4,1)S(1)}, pred[64,4]{1,0:T(8,128)(4,1)}, u32[]{:S(2)}) copy-start(pred[64,4]{1,0:T(8,128)(4,1)} %copy-done.35) | copy-start | bytes 772
  45.4 239.9 %all-reduce.10.cloned.1.call-start = ((), (), s32[]{:S(2)}) async-start(), calls=%async_computation.1 | async-start | bytes 1196032 | tf_op jit(solution)/shard_map/psum | solution.py:132
  48.6 6.0 %slice-start.3 = ((s8[8388608]{0:T(1024)(128)(4,1)}), s8[4194304]{0:T(1024)(128)(4,1)S(1)}, s32[]{:S(2)}) async-start(s8[8388608]{0:T(1024)(128)(4,1)} %bitcast.339), calls=%async_computation.5 | async-start | bytes 8388608
  159.6 6.6 %copy-start.34 = (pred[256]{0:T(512)(128)(4,1)S(1)}, pred[256]{0:T(512)(128)(4,1)}, u32[]{:S(2)}) copy-start(pred[256]{0:T(512)(128)(4,1)} %copy-done.32) | copy-start | bytes 772
  166.1 7.0 %copy-start.16 = (f32[64,2,8,128]{3,2,1,0:T(8,128)S(1)}, f32[64,2,8,128]{3,2,1,0:T(8,128)}, u32[]{:S(2)}) copy-start(f32[64,2,8,128]{3,2,1,0:T(8,128)} %copy-done.15) | copy-start | bytes 1572868
  168.2 6.0 %slice-start.6 = ((s8[8388608]{0:T(1024)(128)(4,1)}), s8[4194304]{0:T(1024)(128)(4,1)S(1)}, s32[]{:S(2)}) async-start(s8[8388608]{0:T(1024)(128)(4,1)} %bitcast.345), calls=%async_computation.8 | async-start | bytes 8388608
  168.2 6.0 %copy-start.39 = (pred[64,4]{1,0:T(8,128)(4,1)S(1)}, pred[64,4]{1,0:T(8,128)(4,1)}, u32[]{:S(2)}) copy-start(pred[64,4]{1,0:T(8,128)(4,1)} %copy-done.35) | copy-start | bytes 772
  168.2 6.0 %slice-start.7 = ((s8[8388608]{0:T(1024)(128)(4,1)}), s8[4194304]{0:T(1024)(128)(4,1)S(1)}, s32[]{:S(2)}) async-start(s8[8388608]{0:T(1024)(128)(4,1)} %bitcast.345), calls=%async_computation.9 | async-start | bytes 8388608
  188.6 96.7 %copy-start.5 = (f32[149504]{0:T(1024)S(1)}, f32[149504]{0:T(1024)}, u32[]{:S(2)}) copy-start(f32[149504]{0:T(1024)} %reshape.216) | copy-start | bytes 1794052
  190.7 96.6 %copy-start.11 = (f32[16,6144]{1,0:T(8,128)S(1)}, f32[16,6144]{1,0:T(8,128)}, u32[]{:S(2)}) copy-start(f32[16,6144]{1,0:T(8,128)} %copy-done.10) | copy-start | bytes 1179652
  190.7 97.6 %copy-start.43 = (f32[16]{0:T(128)S(1)}, f32[16]{0:T(128)}, u32[]{:S(2)}) copy-start(f32[16]{0:T(128)} %get-tuple-element.19) | copy-start | bytes 196
  190.7 97.6 %copy-start.44 = (f32[16]{0:T(128)S(1)}, f32[16]{0:T(128)}, u32[]{:S(2)}) copy-start(f32[16]{0:T(128)} %get-tuple-element.7) | copy-start | bytes 196
  190.7 97.6 %copy-start.45 = (f32[16]{0:T(128)S(1)}, f32[16]{0:T(128)}, u32[]{:S(2)}) copy-start(f32[16]{0:T(128)} %get-tuple-element.8) | copy-start | bytes 196
  190.7 97.6 %copy-start.46 = (f32[16]{0:T(128)S(1)}, f32[16]{0:T(128)}, u32[]{:S(2)}) copy-start(f32[16]{0:T(128)} %get-tuple-element.9) | copy-start | bytes 196
  190.7 97.6 %copy-start.47 = (f32[16]{0:T(128)S(1)}, f32[16]{0:T(128)}, u32[]{:S(2)}) copy-start(f32[16]{0:T(128)} %get-tuple-element.10) | copy-start | bytes 196
  192.2 129.1 %copy-start.14 = (f32[16,8192]{1,0:T(8,128)}, f32[16,8192]{1,0:T(8,128)S(1)}, u32[]{:S(2)}) copy-start(f32[16,8192]{1,0:T(8,128)S(1)} %fusion.22) | copy-start | bytes 1572868
  (39 other events, 160.4 us)
Sparse Core Ops, SparseCore 0:
  45.5 93.1 all-reduce.7
  194.5 90.8 all-reduce.9
where the time goes:
time: 332 us; the launch traced here: 328 us
  waiting for transfers between devices  137 us (41%)
  blocking collectives  59.8 us (18%)
  matrix products  54.7 us (16%)
  local copies, waits for them, and re-layouts  31.1 us (9%)
  other arithmetic  29.9 us (9%)
  between operations  15.2 us (5%)
    psum x2, waiting for transfers between devices, shards(): mean_values = lax.psum(flat_sums, 'bundle') / weight_flat  137 us
    psum x1, blocking collectives, shards(): node_totals = lax.psum(local_weights, 'bundle')  30.6 us
    psum x1, blocking collectives, shards(): gap_terms.append(lax.psum(gap_term, 'bundle'))  29.3 us
    dot_general x5, matrix products, forward(): jnp.einsum('rkij,srkj->sri', grouped_tiles, picked, preferred_element_typ...  25.4 us
    dot_general x6, matrix products, backward(): jnp.einsum('rkij,sri->srkj', grouped_tiles, blocks, preferred_element_typ...  15.9 us
    gather x1, local copies, waits for them, and re-layouts, shards(): jnp.take(matrix_tiles, tile_order, axis=0)  12 us
    dot_general x6, matrix products, backward(): jnp.einsum('vt,stj->svj', cols_onehot, product, precision=lax.Precision.H...  7.83 us
    select_n x6, other arithmetic, forward(): jnp.take(blocks, sorted_cols, axis=1)  7.16 us
  transfers between devices with their start and end apart: 2, of which 2 were waited for; matrix products, arithmetic and copies ran while one was open for 5% of the time, Pallas kernels for 0%

commit v1 on v0

--- a/solution.py
+++ b/solution.py
@@ -1,6 +1,10 @@
+import functools
+
 import jax
 import jax.numpy as jnp
 from jax import lax
+from jax.experimental import pallas as pl
+from jax.experimental.pallas import tpu as pltpu
 from jax.sharding import PartitionSpec as P
 
 NODES2 = 8
@@ -46,7 +50,7 @@
     return summed.reshape(batch_size, -1)
 
 
-def shards(
+def general(
     objective,
     demands,
     multipliers,
@@ -168,6 +172,532 @@
     return (primal, weights_now, hedging_gap, lagrange_bound)
 
 
+MESH = pl.DeviceIdType.MESH
+ROW_TILE, ROW_COL, COL_TILE, COL_ROW, COL_KEEP, COL_LAST = range(6)
+HIGHEST = lax.Precision.HIGHEST
+
+
+def tables(tile_row, tile_col, var_blocks):
+    count = tile_row.shape[0]
+    place = jnp.arange(count, dtype=jnp.int32)
+    keys = jnp.stack([tile_row, tile_col]) * count + place
+    rank = jnp.sum((keys[:, None, :] < keys[:, :, None]).astype(jnp.int32), axis=2)
+    code = place + count * (tile_row + 256 * tile_col)
+    hit = rank[:, :, None] == place[None, None, :]
+    packed = jnp.sum(jnp.where(hit, code[None, :, None], 0), axis=1)
+    tile = packed % count
+    row = (packed // count) % 256
+    col = packed // (count * 256)
+    keep = jnp.concatenate([jnp.zeros(1, jnp.int32), (col[1, 1:] == col[1, :-1]).astype(jnp.int32)])
+    block = jnp.arange(count, dtype=jnp.int32)
+    upto = jnp.sum((tile_col[None, :] <= block[:, None]).astype(jnp.int32), axis=1)
+    own = jnp.any(tile_col[None, :] == block[:, None], axis=1)
+    last = jnp.where(own, upto - 1, count)
+    return jnp.concatenate([tile[0], col[0], tile[1], row[1], keep, last])
+
+
+def mega(
+    parts,
+    idx_ref,
+    objective_ref,
+    demands_ref,
+    mult_ref,
+    kind_ref,
+    meta_ref,
+    tiles_hbm,
+    x_out,
+    w_out,
+    scalars_out,
+    tiles,
+    x,
+    y,
+    xs,
+    ys,
+    q,
+    h,
+    a,
+    h2,
+    a2,
+    runs,
+    runs2,
+    meta_all,
+    mask2,
+    mask3,
+    put1,
+    got1,
+    put2,
+    got2,
+    back1,
+    ret1,
+    back2,
+    ret2,
+    tile_sem,
+    meta_send,
+    meta_recv,
+    put_send,
+    put_recv,
+    ret_send,
+    ret_recv,
+):
+    me = lax.axis_index("bundle")
+    blocks = x.shape[0]
+    rows = x.shape[1]
+    count = tiles.shape[0]
+    con_blocks = y.shape[0]
+    per_row = count // con_blocks
+    free = blocks - 3 * parts
+
+    tile_copy = pltpu.make_async_copy(tiles_hbm, tiles, tile_sem)
+    tile_copy.start()
+
+    barrier = pltpu.get_barrier_semaphore()
+
+    def greet(k, carry):
+        pl.semaphore_signal(
+            barrier, inc=1, device_id={"bundle": lax.rem(me + k, parts)}, device_id_type=MESH
+        )
+        return carry
+
+    lax.fori_loop(1, parts, greet, 0)
+
+    def lanes(block):
+        return pl.ds(pl.multiple_of(block * 128, 128), 128)
+
+    def upper(block):
+        return jnp.where(kind_ref[:, lanes(block)] == 1, 1.0, 3.0).astype(jnp.float32)
+
+    def index(table, item):
+        return idx_ref[table * count + item]
+
+    def first(block, with_w):
+        linear = objective_ref[:, lanes(block)]
+        if with_w:
+            linear = linear + mult_ref[:, lanes(block)]
+        q[block] = linear
+        moved = jnp.clip(-step_tau * linear, 0.0, upper(block))
+        x[block] = moved
+        h[block] = (2.0 * moved).astype(jnp.bfloat16)
+
+    def loop(start, stop, width, body):
+        def many(i, carry):
+            for u in range(width):
+                body(start + i * width + u)
+            return carry
+
+        lax.fori_loop(0, (stop - start) // width, many, 0)
+
+    loop(0, 3 * parts, 4, lambda block: first(block, True))
+    loop(3 * parts, blocks, 4, lambda block: first(block, False))
+
+    pl.semaphore_wait(barrier, parts - 1)
+
+    def meta_copy(k):
+        return pltpu.make_async_remote_copy(
+            src_ref=meta_ref,
+            dst_ref=meta_all.at[me],
+            send_sem=meta_send.at[k],
+            recv_sem=meta_recv.at[k],
+            device_id={"bundle": lax.rem(me + k, parts)},
+            device_id_type=MESH,
+        )
+
+    def put_copy(k, put, got, turn):
+        peer = lax.rem(me + k, parts)
+        return pltpu.make_async_remote_copy(
+            src_ref=put.at[peer],
+            dst_ref=got.at[me],
+            send_sem=put_send.at[turn, k],
+            recv_sem=put_recv.at[turn, k],
+            device_id={"bundle": peer},
+            device_id_type=MESH,
+        )
+
+    def ret_copy(k, back, ret, turn):
+        peer = lax.rem(me + k, parts)
+        return pltpu.make_async_remote_copy(
+            src_ref=back.at[peer],
+            dst_ref=ret.at[me],
+            send_sem=ret_send.at[turn, k],
+            recv_sem=ret_recv.at[turn, k],
+            device_id={"bundle": peer},
+            device_id_type=MESH,
+        )
+
+    def each(body):
+        def step(k, carry):
+            body(k)
+            return carry
+
+        lax.fori_loop(1, parts, step, 0)
+
+    each(lambda k: meta_copy(k).start())
+    meta_all[me] = meta_ref[...]
+
+    def forward(vec, done):
+        def row(r):
+            picked = [vec[index(ROW_COL, r * per_row + k)] for k in range(per_row)]
+            mats = [tiles[index(ROW_TILE, r * per_row + k)] for k in range(per_row)]
+            image = lax.dot_general(
+                jnp.concatenate(picked, axis=1),
+                jnp.concatenate(mats, axis=1),
+                (((1,), (1,)), ((), ())),
+                preferred_element_type=jnp.float32,
+            )
+            done(r, image)
+
+        loop(0, con_blocks, 4, row)
+
+    def backward(vec, into):
+        into[count] = jnp.zeros(into.shape[1:], jnp.float32)
+
+        def many(i, total):
+            for u in range(8):
+                t = i * 8 + u
+                product = jnp.dot(
+                    vec[index(COL_ROW, t)],
+                    tiles[index(COL_TILE, t)],
+                    preferred_element_type=jnp.float32,
+                )
+                total = jnp.where(index(COL_KEEP, t) == 1, total, 0.0) + product
+                into[t] = total
+            return total
+
+        lax.fori_loop(0, count // 8, many, jnp.zeros(into.shape[1:], jnp.float32))
+
+    tile_copy.wait()
+
+    def dual_first(r, image):
+        new = jnp.maximum(step_sigma * (image - demands_ref[:, lanes(r)]), 0.0)
+        y[r] = new
+        a[r] = new.astype(jnp.bfloat16)
+
+    forward(h, dual_first)
+    backward(a, runs)
+
+    def second(block):
+        old = x[block]
+        gradient = q[block] + runs[index(COL_LAST, block)]
+        moved = jnp.clip(old - step_tau * gradient, 0.0, upper(block))
+        x[block] = moved
+        h[block] = (2.0 * moved - old).astype(jnp.bfloat16)
+        return moved
+
+    def scatter(update, put, got, turn):
+        def column(owner):
+            for section in range(3):
+                put[owner, section * rows : (section + 1) * rows, :] = update(
+                    section * parts + owner
+                )
+
+        def send(k):
+            column(lax.rem(me + k, parts))
+            put_copy(k, put, got, turn).start()
+
+        each(send)
+        column(me)
+        got[me] = put[me]
+
+    scatter(second, put1, got1, 0)
+    loop(3 * parts, blocks, 4, second)
+
+    each(lambda k: meta_copy(k).wait_recv())
+    table = meta_all[...].reshape(parts * rows, 128)
+    across = table.T
+    leaf_col, p_col, two_col = table[:, 0:1], table[:, 1:2], table[:, 2:3]
+    leaf_row, p_row, two_row = across[0:1, :], across[1:2, :], across[2:3, :]
+    mask3[...] = jnp.where(leaf_col == leaf_row, p_row, 0.0)
+    mask2[...] = jnp.where(two_col == two_row, p_row, 0.0)
+
+    def dual_second(r, image):
+        new = jnp.maximum(y[r] + step_sigma * (image - demands_ref[:, lanes(r)]), 0.0)
+        y[r] = new
+        a[r] = new.astype(jnp.bfloat16)
+
+    forward(h, dual_second)
+    backward(a, runs)
+
+    my_p = meta_ref[:, 1:2]
+
+    def bound(primal, dual, carry_runs):
+        def body(i, total):
+            for u in range(4):
+                block = i * 4 + u
+                total = total + (
+                    (q[block] + carry_runs[index(COL_LAST, block)]) * primal(block)
+                    - demands_ref[:, lanes(block)] * dual(block)
+                )
+            return total
+
+        total = lax.fori_loop(0, blocks // 4, body, jnp.zeros((rows, 128), jnp.float32))
+        return jnp.sum(my_p * total, axis=0, keepdims=True)
+
+    bound_first = bound(lambda block: x[block], lambda block: y[block], runs)
+
+    def consensus(put, got, back, ret, bound_row, turn):
+        each(lambda k: put_copy(k, put, got, turn).wait_recv())
+        everyone = meta_all[...].reshape(parts * rows, 128)
+        prob = everyone[:, 1:2]
+        one, two, three = [
+            got[:, section * rows : (section + 1) * rows, :].reshape(parts * rows, 128)
+            for section in range(3)
+        ]
+        weights3, weights2 = mask3[...], mask2[...]
+        mean3 = jnp.dot(weights3, three, precision=HIGHEST) / jnp.sum(
+            weights3, axis=1, keepdims=True
+        )
+        mean2 = jnp.dot(weights2, two, precision=HIGHEST) / jnp.sum(
+            weights2, axis=1, keepdims=True
+        )
+        mean1 = jnp.sum(prob * one, axis=0, keepdims=True) / jnp.sum(prob, keepdims=True)
+        square = (three - mean3) ** 2 + (two - mean2) ** 2 + (one - mean1) ** 2
+        gap_row = jnp.sum(prob * square, axis=0, keepdims=True)
+        back[:, 0:rows, :] = mean3.reshape(parts, rows, 128)
+        back[:, rows : 2 * rows, :] = mean2.reshape(parts, rows, 128)
+        line = lax.broadcasted_iota(jnp.int32, (8, 128), 0)
+        extra = jnp.where(
+            line == 0, mean1, jnp.where(line == 1, gap_row, jnp.where(line == 2, bound_row, 0.0))
+        )
+        back[:, 2 * rows :, :] = jnp.broadcast_to(extra[None], (parts, 8, 128))
+        each(lambda k: ret_copy(k, back, ret, turn).start())
+        ret[me] = back[me]
+        each(lambda k: ret_copy(k, back, ret, turn).wait_recv())
+
+    def drain(put, got, back, ret, turn):
+        each(lambda k: put_copy(k, put, got, turn).wait_send())
+        each(lambda k: ret_copy(k, back, ret, turn).wait_send())
+
+    def agreed(ret, section, owner):
+        if section == 0:
+            return ret[owner, 2 * rows : 2 * rows + 1, :]
+        if section == 1:
+            return ret[owner, rows : 2 * rows, :]
+        return ret[owner, 0:rows, :]
+
+    consensus(put1, got1, back1, ret1, bound_first, 0)
+
+    def third(block, section, owner):
+        old = x[block]
+        linear = q[block]
+        carry = runs[index(COL_LAST, block)]
+        limit = upper(block)
+        if section is None:
+            moved = jnp.clip(old - step_tau * (linear + carry), 0.0, limit)
+            spoke = moved
+        else:
+            mean = agreed(ret1, section, owner)
+            half = penalty * (old - mean)
+            w = mult_ref[:, lanes(block)] + half
+            w_out[:, lanes(block)] = w
+            linear = objective_ref[:, lanes(block)] + w
+            q[block] = linear
+            gradient = linear + carry
+            moved = jnp.clip(old - step_tau * (gradient + half), 0.0, limit)
+            spoke = jnp.clip(old - step_tau * gradient, 0.0, limit)
+        x[block] = moved
+        xs[block] = spoke
+        h2[block] = jnp.concatenate(
+            [2.0 * moved - old, 2.0 * spoke - old], axis=0
+        ).astype(jnp.bfloat16)
+
+    def sections(body):
+        def step(owner):
+            for section in range(3):
+                body(section * parts + owner, section, owner)
+
+        loop(0, parts, 2, step)
+
+    sections(third)
+    loop(3 * parts, blocks, 4, lambda block: third(block, None, None))
+
+    def dual_third(r, image):
+        old = y[r]
+        right = demands_ref[:, lanes(r)]
+        hub = jnp.maximum(old + step_sigma * (image[0:rows] - right), 0.0)
+        spoke = jnp.maximum(old + step_sigma * (image[rows:] - right), 0.0)
+        ys[r] = spoke
+        a2[r] = jnp.concatenate([hub, spoke], axis=0).astype(jnp.bfloat16)
+
+    forward(h2, dual_third)
+    backward(a2, runs2)
+
+    def fourth(block, section, owner):
+        both = runs2[index(COL_LAST, block)]
+        linear = q[block]
+        limit = upper(block)
+        old = x[block]
+        gradient = linear + both[0:rows]
+        if section is not None:
+            gradient = gradient + penalty * (old - agreed(ret1, section, owner))
+        moved = jnp.clip(old - step_tau * gradient, 0.0, limit)
+        x_out[:, lanes(block)] = moved
+        old_spoke = xs[block]
+        spoke = jnp.clip(old_spoke - step_tau * (linear + both[rows:]), 0.0, limit)
+        xs[block] = spoke
+        h[block] = (2.0 * spoke - old_spoke).astype(jnp.bfloat16)
+        return moved
+
+    each(lambda k: meta_copy(k).wait_send())
+    drain(put1, got1, back1, ret1, 0)
+
+    def scatter_last():
+        def column(owner):
+            for section in range(3):
+                put2[owner, section * rows : (section + 1) * rows, :] = fourth(
+                    section * parts + owner, section, owner
+                )
+
+        def send(k):
+            column(lax.rem(me + k, parts))
+            put_copy(k, put2, got2, 1).start()
+
+        each(send)
+        column(me)
+        got2[me] = put2[me]
+
+    scatter_last()
+    loop(3 * parts, blocks, 4, lambda block: fourth(block, None, None))
+
+    def dual_fourth(r, image):
+        new = jnp.maximum(ys[r] + step_sigma * (image - demands_ref[:, lanes(r)]), 0.0)
+        ys[r] = new
+        a[r] = new.astype(jnp.bfloat16)
+
+    forward(h, dual_fourth)
+    backward(a, runs)
+    bound_second = bound(lambda block: xs[block], lambda block: ys[block], runs)
+    consensus(put2, got2, back2, ret2, bound_second, 1)
+
+    def finish(block, section, owner):
+        w_out[:, lanes(block)] = w_out[:, lanes(block)] + penalty * (
+            x_out[:, lanes(block)] - agreed(ret2, section, owner)
+        )
+
+    sections(finish)
+    drain(put2, got2, back2, ret2, 1)
+    total = jnp.sum(meta_all[...].reshape(parts * rows, 128)[:, 1:2])
+    gap_scale = 1.0 / (3 * parts * 128 * total)
+    bound_scale = 1.0 / (blocks * 128 * total)
+    for iteration, ret in enumerate((ret1, ret2)):
+        scalars_out[iteration] = jnp.sum(ret[:, 2 * rows + 1 : 2 * rows + 2, :]) * gap_scale
+        scalars_out[2 + iteration] = jnp.sum(ret[:, 2 * rows + 2 : 2 * rows + 3, :]) * bound_scale
+
+
+def shards(
+    parts,
+    objective,
+    demands,
+    multipliers,
+    probability,
+    matrix_tiles,
+    tile_row,
+    tile_col,
+    unit_kind,
+    leaf_node,
+    node_parent,
+):
+    rows, width = objective.shape
+    tile = matrix_tiles.shape[1]
+    section = multipliers.shape[1] // 3
+    count = matrix_tiles.shape[0]
+    fits = (
+        tile == 128
+        and rows == 16
+        and section == parts * tile
+        and width == demands.shape[1]
+        and width // tile <= min(count, 256)
+        and parts > 1
+    )
+    if not fits:
+        return general(
+            objective,
+            demands,
+            multipliers,
+            probability,
+            matrix_tiles,
+            tile_row,
+            tile_col,
+            unit_kind,
+            leaf_node,
+            node_parent,
+        )
+    blocks = width // tile
+    table = tables(tile_row, tile_col, blocks)
+    nodes = jnp.arange(node_parent.shape[0], dtype=jnp.int32)
+    parent = jnp.sum(
+        jnp.where(leaf_node[:, None] == nodes[None, :], node_parent[None, :], 0), axis=1
+    )
+    lane = jnp.arange(tile)[None, :]
+    meta = jnp.where(
+        lane == 0,
+        leaf_node[:, None].astype(jnp.float32),
+        jnp.where(
+            lane == 1,
+            probability[:, None],
+            jnp.where(lane == 2, parent[:, None].astype(jnp.float32), 0.0),
+        ),
+    )
+    f32, bf16 = jnp.float32, jnp.bfloat16
+    state = pltpu.VMEM((blocks, rows, tile), f32)
+    vec = pltpu.VMEM((blocks, rows, tile), bf16)
+    vec2 = pltpu.VMEM((blocks, 2 * rows, tile), bf16)
+    put = pltpu.VMEM((parts, 3 * rows, tile), f32)
+    ret = pltpu.VMEM((parts, 2 * rows + 8, tile), f32)
+    mask = pltpu.VMEM((parts * rows, parts * rows), f32)
+    sems = pltpu.SemaphoreType.DMA((2, parts))
+    vmem = pl.BlockSpec(memory_space=pltpu.VMEM)
+    smem = pl.BlockSpec(memory_space=pltpu.SMEM)
+    flops = 2 * count * tile * tile * rows * 10
+    solution_x, new_w, scalars = pl.pallas_call(
+        functools.partial(mega, parts),
+        out_shape=(
+            jax.ShapeDtypeStruct((rows, width), f32),
+            jax.ShapeDtypeStruct(multipliers.shape, f32),
+            jax.ShapeDtypeStruct((4,), f32),
+        ),
+        in_specs=[smem, vmem, vmem, vmem, vmem, vmem, pl.BlockSpec(memory_space=pl.ANY)],
+        out_specs=(vmem, vmem, smem),
+        scratch_shapes=[
+            pltpu.VMEM(matrix_tiles.shape, bf16),
+            state,
+            state,
+            state,
+            state,
+            state,
+            vec,
+            vec,
+            vec2,
+            vec2,
+            pltpu.VMEM((count + 1, rows, tile), f32),
+            pltpu.VMEM((count + 1, 2 * rows, tile), f32),
+            pltpu.VMEM((parts, rows, tile), f32),
+            mask,
+            mask,
+            put,
+            put,
+            put,
+            put,
+            ret,
+            ret,
+            ret,
+            ret,
+            pltpu.SemaphoreType.DMA,
+            pltpu.SemaphoreType.DMA((parts,)),
+            pltpu.SemaphoreType.DMA((parts,)),
+            sems,
+            sems,
+            sems,
+            sems,
+        ],
+        compiler_params=pltpu.CompilerParams(
+            collective_id=0, has_side_effects=True, vmem_limit_bytes=48 * 1024 * 1024
+        ),
+        cost_estimate=pl.CostEstimate(
+            flops=flops, bytes_accessed=count * tile * tile * 2 + rows * width * 20, transcendentals=0
+        ),
+    )(table, objective, demands, multipliers, unit_kind.reshape(1, width), meta, matrix_tiles)
+    return solution_x, new_w, scalars[:2], scalars[2:]
+
+
 def solution(mesh):
     in_specs = (
         P(("groups", "bundle"), None),
@@ -187,4 +717,4 @@
         P("groups"),
         P("groups"),
     )
-    return jax.shard_map(shards, mesh=mesh, in_specs=in_specs, out_specs=out_specs, check_vma=False)
+    return jax.shard_map(functools.partial(shards, mesh.shape["bundle"]), mesh=mesh, in_specs=in_specs, out_specs=out_specs, check_vma=False)

time: 332 us -> 82.9 us (0.25)
  waiting for transfers between devices: 137 us -> 0 us
  Pallas kernels: 0 us -> 69 us
  blocking collectives: 59.8 us -> 0 us
  matrix products: 54.7 us -> 0 us
  local copies, waits for them, and re-layouts: 31.1 us -> 6.04 us
  other arithmetic: 29.9 us -> 5.81 us
  between operations: 15.2 us -> 0.72 us
    psum x2 -> x0, waiting for transfers between devices: 137 us -> none  [shards(): mean_values = lax.psum(flat_sums, 'bundle') / weight_flat]
    pallas_call x0 -> x1, Pallas kernels: none -> 69 us  [shards(): pl.pallas_call(functools.partial(mega, parts), out_shape=(jax.ShapeDtypeS...]
    psum x2 -> x0, blocking collectives: 59.8 us -> none  [the longest x1 30.6 us: shards(): node_totals = lax.psum(local_weights, 'bundle')]
    dot_general x30 -> x0, matrix products: 54.7 us -> none  [the longest x5 25.4 us: forward(): jnp.einsum('rkij,srkj->sri', grouped_tiles, picked, preferred_element_typ...]
    gather x7 -> x0, local copies, waits for them, and re-layouts: 20.7 us -> none  [the longest x1 12 us: shards(): jnp.take(matrix_tiles, tile_order, axis=0)]
    select_n x8 -> x4, other arithmetic: 7.17 us -> 0.76 us  [the longest x1 0.73 us: shards(): jnp.where(lane == 0, leaf_node[:, None].astype(jnp.float32), jnp.where(la...]
    div x3 -> x0, other arithmetic: 5.54 us -> none  [the longest x1 3.06 us: shards(): hedging_gap = gap_totals / (3 * section_width * total_prob)]
    reduce_sum x5 -> x4, other arithmetic: 6.04 us -> 2.08 us  [the longest x1 0.85 us: shards(): jnp.sum(jnp.where(leaf_node[:, None] == nodes[None, :], node_parent[None,...]
  transfers between devices with their start and end apart: 2 -> 0, of which waited for: 2 -> 0; matrix products, arithmetic and copies ran while one was open for 5% -> 0% of each run, Pallas kernels for 0% -> 0%
where the time goes in v1:
time: 82.9 us; the launch traced here: 81.5 us
  Pallas kernels  69 us (83%)
  local copies, waits for them, and re-layouts  6.04 us (7%)
  other arithmetic  5.81 us (7%)
    pallas_call x1, Pallas kernels, shards(): pl.pallas_call(functools.partial(mega, parts), out_shape=(jax.ShapeDtypeS...  69 us
    unnamed x10, local copies, waits for them, and re-layouts  5.37 us

profile of v1, /device:TPU:1, one launch (start us, length us, event | category | flops | bytes accessed | tf_op | source)
XLA Modules:
  0.0 81.5 jit_solution(15027555622712099115)
XLA Ops:
  0.6 0.9 %select_reduce_fusion.1 = s32[16]{0:T(128)S(1)} fusion(s32[64]{0:T(128)} %param.19, s32[16]{0:T(128)} %param.18), kind=kLoop, calls=%fused_computation.8 | loop fusion | flops 3056 | bytes 384 | tf_op jit(solution)/shard_map/reduce_sum | solution.py:626
  1.5 0.7 convert_element_type.28
  2.2 0.8 fusion
  3.0 0.7 multiply_add_fusion
  3.7 0.8 convert_reduce_fusion.1
  4.5 0.7 fusion.1
  5.2 0.2 convert_reduce_fusion
  5.4 0.2 select_reduce_fusion
  5.7 0.1 compare_convert_fusion
  5.8 0.1 concatenate.11.idx_ref
  5.9 0.7 select_select_fusion.meta_ref
  6.6 0.0 copy-start
  6.6 1.0 %copy-done = f32[16,8192]{1,0:T(8,128)S(1)} copy-done((f32[16,8192]{1,0:T(8,128)S(1)}, f32[16,8192]{1,0:T(8,128)}, u32[]{:S(2)}) %copy-start) | copy-done | bytes 524312
  7.6 0.0 copy-start.1
  7.6 1.0 %copy-done.1 = f32[16,8192]{1,0:T(8,128)S(1)} copy-done((f32[16,8192]{1,0:T(8,128)S(1)}, f32[16,8192]{1,0:T(8,128)}, u32[]{:S(2)}) %copy-start.1) | copy-done | bytes 524312
  8.7 0.0 copy-start.2
  8.7 1.0 %copy-done.2 = f32[16,6144]{1,0:T(8,128)S(1)} copy-done((f32[16,6144]{1,0:T(8,128)S(1)}, f32[16,6144]{1,0:T(8,128)}, u32[]{:S(2)}) %copy-start.2) | copy-done | bytes 393240
  9.7 0.0 copy-start.3
  9.7 0.8 copy-done.3
  10.4 69.0 %shard_map.129 = (f32[16,8192]{1,0:T(8,128)S(1)}, f32[16,6144]{1,0:T(8,128)S(1)}, f32[4]{0:T(128)S(1)}) custom-call(s32[1536]{0:T(1024)S(1)} %concatenate.11.idx_ref, f32[16,8192]{1,0:T(8,128)S(1)} %copy-done, f32[16,8192]{1,0:T(8,128)S(1)} %copy-done.1, f32[16,6144]{1,0:T(8,128)S(1)} %copy-done.2, s32[1,8192]{1,0:T(1,128)S(1)} %bitcast.8, ...), custom_call_target="tpu_custom_call" | custom-call | flops 1342177280 | bytes 11010048 | tf_op jit(solution)/shard_map/pallas_call | solution.py:650
  79.4 0.6 fusion.3
  80.0 0.8 copy.16
  80.8 0.7 copy.17
  (10 shorter events, 0.1 us)
Async XLA Ops:
  6.6 1.0 %copy-start = (f32[16,8192]{1,0:T(8,128)S(1)}, f32[16,8192]{1,0:T(8,128)}, u32[]{:S(2)}) copy-start(f32[16,8192]{1,0:T(8,128)} %objective_ref.1) | copy-start | bytes 1572868
  7.6 1.0 %copy-start.1 = (f32[16,8192]{1,0:T(8,128)S(1)}, f32[16,8192]{1,0:T(8,128)}, u32[]{:S(2)}) copy-start(f32[16,8192]{1,0:T(8,128)} %demands_ref.1) | copy-start | bytes 1572868
  8.7 1.0 %copy-start.2 = (f32[16,6144]{1,0:T(8,128)S(1)}, f32[16,6144]{1,0:T(8,128)}, u32[]{:S(2)}) copy-start(f32[16,6144]{1,0:T(8,128)} %mult_ref.1) | copy-start | bytes 1179652
  9.7 0.8 copy-start.3

commit v2 on v1

--- a/solution.py
+++ b/solution.py
@@ -286,8 +286,8 @@
 
         lax.fori_loop(0, (stop - start) // width, many, 0)
 
-    loop(0, 3 * parts, 4, lambda block: first(block, True))
-    loop(3 * parts, blocks, 4, lambda block: first(block, False))
+    loop(0, 3 * parts, 8, lambda block: first(block, True))
+    loop(3 * parts, blocks, 8, lambda block: first(block, False))
 
     pl.semaphore_wait(barrier, parts - 1)
 
@@ -345,14 +345,14 @@
             )
             done(r, image)
 
-        loop(0, con_blocks, 4, row)
+        loop(0, con_blocks, 16, row)
 
     def backward(vec, into):
         into[count] = jnp.zeros(into.shape[1:], jnp.float32)
 
         def many(i, total):
-            for u in range(8):
-                t = i * 8 + u
+            for u in range(32):
+                t = i * 32 + u
                 product = jnp.dot(
                     vec[index(COL_ROW, t)],
                     tiles[index(COL_TILE, t)],
@@ -362,7 +362,7 @@
                 into[t] = total
             return total
 
-        lax.fori_loop(0, count // 8, many, jnp.zeros(into.shape[1:], jnp.float32))
+        lax.fori_loop(0, count // 32, many, jnp.zeros(into.shape[1:], jnp.float32))
 
     tile_copy.wait()
 
@@ -398,7 +398,7 @@
         got[me] = put[me]
 
     scatter(second, put1, got1, 0)
-    loop(3 * parts, blocks, 4, second)
+    loop(3 * parts, blocks, 8, second)
 
     each(lambda k: meta_copy(k).wait_recv())
     table = meta_all[...].reshape(parts * rows, 128)
@@ -420,15 +420,15 @@
 
     def bound(primal, dual, carry_runs):
         def body(i, total):
-            for u in range(4):
-                block = i * 4 + u
+            for u in range(8):
+                block = i * 8 + u
                 total = total + (
                     (q[block] + carry_runs[index(COL_LAST, block)]) * primal(block)
                     - demands_ref[:, lanes(block)] * dual(block)
                 )
             return total
 
-        total = lax.fori_loop(0, blocks // 4, body, jnp.zeros((rows, 128), jnp.float32))
+        total = lax.fori_loop(0, blocks // 8, body, jnp.zeros((rows, 128), jnp.float32))
         return jnp.sum(my_p * total, axis=0, keepdims=True)
 
     bound_first = bound(lambda block: x[block], lambda block: y[block], runs)
@@ -504,10 +504,10 @@
             for section in range(3):
                 body(section * parts + owner, section, owner)
 
-        loop(0, parts, 2, step)
+        loop(0, parts, 4, step)
 
     sections(third)
-    loop(3 * parts, blocks, 4, lambda block: third(block, None, None))
+    loop(3 * parts, blocks, 8, lambda block: third(block, None, None))
 
     def dual_third(r, image):
         old = y[r]
@@ -555,7 +555,7 @@
         got2[me] = put2[me]
 
     scatter_last()
-    loop(3 * parts, blocks, 4, lambda block: fourth(block, None, None))
+    loop(3 * parts, blocks, 8, lambda block: fourth(block, None, None))
 
     def dual_fourth(r, image):
         new = jnp.maximum(ys[r] + step_sigma * (image - demands_ref[:, lanes(r)]), 0.0)

time: 82.9 us -> 72 us (0.87); the launches traced: 81.5 us -> 71.6 us
  Pallas kernels: 69 us -> 59 us
    pallas_call x1, Pallas kernels: 69 us -> 59 us  [shards(): pl.pallas_call(functools.partial(mega, parts), out_shape=(jax.ShapeDtypeS...]
where the time goes in v2:
time: 72 us; the launch traced here: 71.6 us
  Pallas kernels  59 us (82%)
  local copies, waits for them, and re-layouts  6.04 us (8%)
  other arithmetic  5.81 us (8%)
  between operations  0.72 us (1%)
    pallas_call x1, Pallas kernels, shards(): pl.pallas_call(functools.partial(mega, parts), out_shape=(jax.ShapeDtypeS...  59 us
    unnamed x10, local copies, waits for them, and re-layouts  5.37 us

profile of v2, /device:TPU:1, one launch (start us, length us, event | category | flops | bytes accessed | tf_op | source)
XLA Modules:
  0.0 71.6 jit_solution(2365736918745819577)
XLA Ops:
  0.6 0.9 %select_reduce_fusion.1 = s32[16]{0:T(128)S(1)} fusion(s32[64]{0:T(128)} %param.19, s32[16]{0:T(128)} %param.18), kind=kLoop, calls=%fused_computation.8 | loop fusion | flops 3056 | bytes 384 | tf_op jit(solution)/shard_map/reduce_sum | solution.py:626
  1.5 0.7 convert_element_type.28
  2.2 0.8 %fusion = pred[256]{0:T(512)(128)(4,1)S(1)} fusion(s32[256]{0:T(256)} %param.16), kind=kLoop, calls=%fused_computation.6 | loop fusion | flops 130816 | bytes 1280 | tf_op jit(solution)/shard_map/reduce_or | solution.py:194
  3.0 0.7 multiply_add_fusion
  3.7 0.8 %convert_reduce_fusion.1 = s32[256]{0:T(256)S(1)} fusion(s32[256]{0:T(256)} %param.16), kind=kLoop, calls=%fused_computation.3 | loop fusion | flops 196352 | bytes 2048 | tf_op jit(solution)/shard_map/reduce_sum | solution.py:193
  4.5 0.7 fusion.1
  5.2 0.2 convert_reduce_fusion
  5.4 0.2 select_reduce_fusion
  5.7 0.1 compare_convert_fusion
  5.8 0.1 concatenate.11.idx_ref
  5.9 0.7 %select_select_fusion.meta_ref = f32[16,128]{1,0:T(8,128)S(1)} fusion(f32[16]{0:T(128)S(1)} %convert_element_type.29, f32[16]{0:T(128)} %param.13, f32[16]{0:T(128)S(1)} %convert_element_type.28, pred[128]{0:T(512)(128)(4,1)S(1)} %get-tuple-element.18, pred[128]{0:T(512)(128)(4,1)S(1)} %get-tuple-element.19, pred[128]{0:T(512)(128)(4,1)S(1)} %iota_compare_fusion.6), kind=kLoop, calls=%fused_computation.7 | loop fusion | flops 6144 | bytes 8768 | tf_op jit(solution)/shard_map/jit(_where)/select_n | solution.py:630
  6.6 0.0 copy-start
  6.6 1.0 %copy-done = f32[16,8192]{1,0:T(8,128)S(1)} copy-done((f32[16,8192]{1,0:T(8,128)S(1)}, f32[16,8192]{1,0:T(8,128)}, u32[]{:S(2)}) %copy-start) | copy-done | bytes 524312
  7.6 0.0 copy-start.1
  7.6 1.0 %copy-done.1 = f32[16,8192]{1,0:T(8,128)S(1)} copy-done((f32[16,8192]{1,0:T(8,128)S(1)}, f32[16,8192]{1,0:T(8,128)}, u32[]{:S(2)}) %copy-start.1) | copy-done | bytes 524312
  8.7 0.0 copy-start.2
  8.7 1.0 %copy-done.2 = f32[16,6144]{1,0:T(8,128)S(1)} copy-done((f32[16,6144]{1,0:T(8,128)S(1)}, f32[16,6144]{1,0:T(8,128)}, u32[]{:S(2)}) %copy-start.2) | copy-done | bytes 393240
  9.7 0.0 copy-start.3
  9.7 0.8 %copy-done.3 = s32[8192]{0:T(1024)S(1)} copy-done((s32[8192]{0:T(1024)S(1)}, s32[8192]{0:T(1024)}, u32[]{:S(2)}) %copy-start.3) | copy-done | bytes 32792
  10.4 59.0 %shard_map.129 = (f32[16,8192]{1,0:T(8,128)S(1)}, f32[16,6144]{1,0:T(8,128)S(1)}, f32[4]{0:T(128)S(1)}) custom-call(s32[1536]{0:T(1024)S(1)} %concatenate.11.idx_ref, f32[16,8192]{1,0:T(8,128)S(1)} %copy-done, f32[16,8192]{1,0:T(8,128)S(1)} %copy-done.1, f32[16,6144]{1,0:T(8,128)S(1)} %copy-done.2, s32[1,8192]{1,0:T(1,128)S(1)} %bitcast.8, ...), custom_call_target="tpu_custom_call" | custom-call | flops 1342177280 | bytes 11010048 | tf_op jit(solution)/shard_map/pallas_call | solution.py:650
  69.4 0.6 fusion.3
  70.0 0.8 %copy.16 = f32[16,8192]{1,0:T(8,128)} copy(f32[16,8192]{1,0:T(8,128)S(1)} %get-tuple-element.24) | data formatting | bytes 1048576
  70.8 0.7 %copy.17 = f32[16,6144]{1,0:T(8,128)} copy(f32[16,6144]{1,0:T(8,128)S(1)} %get-tuple-element.25) | data formatting | bytes 786432
  (10 shorter events, 0.1 us)
Async XLA Ops:
  6.6 1.0 %copy-start = (f32[16,8192]{1,0:T(8,128)S(1)}, f32[16,8192]{1,0:T(8,128)}, u32[]{:S(2)}) copy-start(f32[16,8192]{1,0:T(8,128)} %objective_ref.1) | copy-start | bytes 1572868
  7.6 1.0 %copy-start.1 = (f32[16,8192]{1,0:T(8,128)S(1)}, f32[16,8192]{1,0:T(8,128)}, u32[]{:S(2)}) copy-start(f32[16,8192]{1,0:T(8,128)} %demands_ref.1) | copy-start | bytes 1572868
  8.7 1.0 %copy-start.2 = (f32[16,6144]{1,0:T(8,128)S(1)}, f32[16,6144]{1,0:T(8,128)}, u32[]{:S(2)}) copy-start(f32[16,6144]{1,0:T(8,128)} %mult_ref.1) | copy-start | bytes 1179652
  9.7 0.8 %copy-start.3 = (s32[8192]{0:T(1024)S(1)}, s32[8192]{0:T(1024)}, u32[]{:S(2)}) copy-start(s32[8192]{0:T(1024)} %param.17) | copy-start | bytes 98308
